TPU v7x, 256 devices: a whole 4x4x8 slice. The times are simulated.
256 devices in a mesh: row: 4 (over x), col: 4 (over y), gz: 16 (over z, core).
Axes of the slice: x: 4, y: 4, z: 8, core: 2. Of those that a mesh axis runs over, the one named last changes fastest.
Arguments:
- col_panels: bfloat16 [16, 8, 4096, 256], P('gz', 'col', 'row'), may hold values from -0.3984375 to 0.3984375
- row_panels: bfloat16 [16, 8, 256, 4096], P('gz', 'row', None, 'col'), may hold values from -0.796875 to 0.796875
- diag_inverse: bfloat16 [16, 8, 256, 256], P('gz', 'col')
- live: int32 [16], P('gz'), may hold values from 1 to 8, as said below
- schur_block: float32 [4096, 4096], P(('row', 'gz'), 'col'), may hold values from -6 to 6
Outputs:
- updated: float32 [4096, 4096], P(('row', 'gz'), 'col')
Inputs may be any that keep to these rules, and one draw needn't show every extreme that they name: Slots 0 to live[z] - 1 of layer z take part; some layer has all 8 slots live.
All inputs are finite; a program needn't handle non-finite values.
Results may differ from a plain program's by a relative error of at most 0.0028.
Values may be sent and summed in bfloat16 or wider, within the bound.
A program may use at most 64 MiB of HBM per device.

v0:
```python
import jax
import jax.numpy as jnp
from jax import lax
from jax.sharding import PartitionSpec as P


def local(col_panels, row_panels, diag_inverse, live, schur_block):
    owned = jnp.einsum(
        "srw,swv->srv", col_panels[0], diag_inverse[0], preferred_element_type=jnp.float32
    ).astype(jnp.bfloat16)
    live_count = live[0]
    uppers = lax.all_gather(row_panels[0], "row", axis=0, tiled=True)
    lowers = lax.all_gather(owned, "col", axis=0, tiled=True)
    keeper = (jnp.arange(lowers.shape[0]) < live_count).astype(jnp.bfloat16)
    lowers = lowers * keeper[:, None, None]
    partial_sum = jnp.einsum("srw,swc->rc", lowers, uppers, preferred_element_type=jnp.float32)
    summed = lax.psum_scatter(partial_sum, "gz", scatter_dimension=0, tiled=True)
    return schur_block - summed


def solution(mesh):
    placed = (
        P("gz", "col", "row", None),
        P("gz", "row", None, "col"),
        P("gz", "col", None, None),
        P("gz"),
        P(("row", "gz"), "col"),
    )
    return jax.shard_map(
        local, mesh=mesh, in_specs=placed, out_specs=P(("row", "gz"), "col"), check_vma=False
    )
```

profile of v0, /device:TPU:1, one launch (start us, length us, event | category | flops | bytes accessed | tf_op | source)
XLA Modules:
  0.0 195.2 jit_solution(4272050347009616832)
XLA Ops:
  6.5 0.0 copy-start
  6.5 0.0 all-gather.6.cloned.1.call-start
  6.5 0.7 all-gather.6.cloned.1.call-update
  7.3 0.0 all-gather.4.cloned.1.call-start
  7.3 0.5 copy-done
  7.8 2.4 %convolution_convert_fusion = bf16[2,1024,256]{2,1,0:T(8,128)(2,1)} fusion(bf16[1,2,1024,256]{3,2,1,0:T(8,128)(2,1)S(1)} %copy-done, bf16[1,2,256,256]{3,2,1,0:T(8,128)(2,1)} %param.7), kind=kOutput, calls=%fused_computation.5 | convolution fusion | flops 268959744 | bytes 2359296 | tf_op jit(solution)/shard_map/srw,swv->srv/dot_general | solution.py:8
  10.2 0.0 all-gather.4.cloned.1.call-update
  10.2 0.0 reduce-scatter.2.cloned.1.call-start
  10.9 52.9 %all-gather.6.cloned.1.call-done = bf16[1,8,256,1024]{3,2,0,1:T(8,128)(2,1)} async-done(((bf16[1,2,256,1024]{3,2,0,1:T(8,128)(2,1)}), bf16[1,8,256,1024]{3,2,0,1:T(8,128)(2,1)}) %all-gather.6.cloned.1.call-update) | async-done | bytes 4194320 | tf_op jit(solution)/shard_map/all_gather | solution.py:12
  63.8 53.1 %all-gather.4.cloned.1.call-done = bf16[8,1024,256]{2,1,0:T(8,128)(2,1)} async-done(((bf16[2,1024,256]{2,1,0:T(8,128)(2,1)}), bf16[8,1024,256]{2,1,0:T(8,128)(2,1)}) %all-gather.4.cloned.1.call-update) | async-done | bytes 4194320 | tf_op jit(solution)/shard_map/all_gather | solution.py:13
  116.9 9.9 %fusion.3 = f32[1024,1024]{1,0:T(8,128)} fusion(bf16[1,8,256,1024]{3,2,0,1:T(8,128)(2,1)} %all-gather.6.cloned.1.call-done, bf16[8,1024,256]{2,1,0:T(8,128)(2,1)} %all-gather.4.cloned.1.call-done, bf16[8]{0:T(256)(128)(2,1)S(1)} %compare_convert_fusion), kind=kOutput, calls=%fused_computation.3 | convolution fusion | flops 4297064448 | bytes 12582928 | tf_op jit(solution)/shard_map/srw,swc->rc/dot_general | solution.py:16
  126.8 0.0 copy-start.1
  126.8 0.0 reduce-scatter.2.cloned.1.call-update
  126.8 60.1 %reduce-scatter.2.cloned.1.call-done = f32[64,1024]{1,0:T(8,128)} async-done(((f32[1024,1024]{1,0:T(8,128)}), f32[64,1024]{1,0:T(8,128)}) %reduce-scatter.2.cloned.1.call-update) | async-done | bytes 262160 | tf_op jit(solution)/shard_map/reduce_scatter | solution.py:17
  187.0 0.0 copy-done.1
  187.0 1.7 sub.3
  (1 shorter events, 0.0 us)
Async XLA Ops:
  6.5 1.2 copy-start
  6.5 57.3 %all-gather.6.cloned.1.call-start = ((), (), s32[]{:S(2)}) async-start(), calls=%async_computation.3 | async-start | bytes 5242880 | tf_op jit(solution)/shard_map/all_gather | solution.py:12
  7.3 109.6 %all-gather.4.cloned.1.call-start = ((), (), s32[]{:S(2)}) async-start(), calls=%async_computation.1 | async-start | bytes 5242880 | tf_op jit(solution)/shard_map/all_gather | solution.py:13
  10.2 176.7 %reduce-scatter.2.cloned.1.call-start = ((), (), s32[]{:S(2)}) async-start(), calls=%async_computation.2 | async-start | bytes 4456448 | tf_op jit(solution)/shard_map/reduce_scatter | solution.py:17
  126.8 60.2 %copy-start.1 = (f32[64,1024]{1,0:T(8,128)S(1)}, f32[64,1024]{1,0:T(8,128)}, u32[]{:S(2)}) copy-start(f32[64,1024]{1,0:T(8,128)} %param.9) | copy-start | bytes 786436
Sparse Core Ops, SparseCore 0:
  9.2 54.5 all-gather.5
  65.6 51.2 all-gather.3
  127.0 59.9 reduce-scatter.1
where the time goes:
time: 198 us; the launch traced here: 195 us
  waiting for transfers between devices  167 us (84%)
  between operations  13.8 us (7%)
  matrix products  12.4 us (6%)
    reduce_scatter x1, waiting for transfers between devices, local(): lax.psum_scatter(partial_sum, 'gz', scatter_dimension=0, tiled=True)  60.1 us
    all_gather x1, waiting for transfers between devices, local(): lowers = lax.all_gather(owned, 'col', axis=0, tiled=True)  53.1 us
    all_gather x1, waiting for transfers between devices, local(): uppers = lax.all_gather(row_panels[0], 'row', axis=0, tiled=True)  52.9 us
    dot_general x1, matrix products, local(): jnp.einsum('srw,swc->rc', lowers, uppers, preferred_element_type=jnp.floa...  9.94 us
  transfers between devices with their start and end apart: 3, of which 3 were waited for; matrix products, arithmetic and copies ran while one was open for 1% of the time, Pallas kernels for 0%

commit v1 on v0

v1 whole, which is shorter than its diff:
```python
import functools

import jax
import jax.numpy as jnp
from jax import lax
from jax.experimental import pallas as pl
from jax.experimental.pallas import tpu as pltpu
from jax.sharding import PartitionSpec as P

MESH = pl.DeviceIdType.MESH
F32 = jnp.float32
BF16 = jnp.bfloat16
PARTS = 4
H = 16
CW = 256
CR = 256


def group_blocks():
    groups = []
    for p in range(PARTS):
        blocks = [(i, p) for i in range(p)] + [(p, j) for j in range(p + 1)]
        if len(blocks) > 5:
            groups.append((p, blocks[:4]))
            groups.append((p, blocks[4:]))
        else:
            groups.append((p, blocks))
    return groups


GROUPS = group_blocks()


def kernel(live_ref, x_hbm, u_hbm, d_hbm, out_ref, *scr):
    scr = list(scr)
    xs, dg, lg = scr[:3]
    del scr[:3]
    ug = [scr.pop(0) for _ in range(PARTS)]
    cx = [scr.pop(0) for _ in GROUPS]
    cr = [scr.pop(0) for _ in GROUPS]
    zs = [scr.pop(0) for _ in GROUPS]
    zr = [scr.pop(0) for _ in GROUPS]
    load_sem, ring_send, ring_recv, core_send, core_recv, z_send, z_recv = scr

    r, c, g = lax.axis_index("row"), lax.axis_index("col"), lax.axis_index("gz")
    z, core = lax.div(g, 2), lax.rem(g, 2)

    def along(axis, d):
        if axis == 0:
            return (lax.rem(r + 4 + d, 4), c, g)
        return (r, lax.rem(c + 4 + d, 4), g)

    other_core = (r, c, 2 * z + 1 - core)

    def z_at(d):
        return lax.rem(z + d, 8)

    def z_dev(d):
        return (r, c, 2 * z_at(d) + core)

    loads = [
        pltpu.make_async_copy(d_hbm, dg, load_sem.at[0]),
        pltpu.make_async_copy(x_hbm, xs, load_sem.at[1]),
    ]
    for t in range(PARTS):
        loads.append(
            pltpu.make_async_copy(
                u_hbm.at[:, :, pl.ds(CW * t, CW)],
                ug[t].at[pl.ds(2 * r, 2)],
                load_sem.at[2 + t],
            )
        )
    for cp in loads:
        cp.start()

    barrier = pltpu.get_barrier_semaphore()
    peers = [along(a, d) for a in (0, 1) for d in (1, -1)]
    peers += [other_core] + [z_dev(d) for d in range(1, 8)]
    for dev in peers:
        pl.semaphore_signal(barrier, inc=1, device_id=dev, device_id_type=MESH)

    def lower(t):
        for s in range(2):
            keep = jnp.where(2 * c + s < live_ref[0], 1.0, 0.0).astype(F32)
            halves = [
                xs[s, :, par, H * t : H * t + H, :].reshape(CR // 2, 256)
                for par in range(2)
            ]
            prod = jnp.dot(
                jnp.concatenate(halves, axis=0), dg[s], preferred_element_type=F32
            )
            lg[2 * c + s, CR * t : CR * t + CR, :] = (prod * keep).astype(BF16)

    def piece(axis, slot, t):
        if axis == 0:
            return ug[t].at[slot]
        return lg.at[slot, pl.ds(CR * t, CR)]

    me = (r, c)
    copies = {}

    def ring_copy(axis, t, way, kind):
        key = (axis, t, way, kind)
        if key not in copies:
            d = 1 if way == 0 else -1
            if kind < 2:
                slot = 2 * me[axis] + kind
            else:
                slot = 2 * lax.rem(me[axis] + 4 - d, 4) + way
            sem = ((axis * PARTS + t) * 2 + way) * 3 + kind
            src = dst = piece(axis, slot, t)
            if axis == 0 and kind < 2:
                src = u_hbm.at[kind, :, pl.ds(CW * t, CW)]
            copies[key] = pltpu.make_async_remote_copy(
                src_ref=src,
                dst_ref=dst,
                send_sem=ring_send.at[sem],
                recv_sem=ring_recv.at[sem],
                device_id=along(axis, d),
                device_id_type=MESH,
            )
        return copies[key]

    def direct(axis, t):
        for n in range(2):
            for way in range(2):
                ring_copy(axis, t, way, n if way == 0 else 1 - n).start()

    def forward(t):
        for axis in range(2):
            for way in range(2):
                ring_copy(axis, t, way, way).wait_recv()
                ring_copy(axis, t, way, 2).start()

    def rest(t):
        for axis in range(2):
            for way in range(2):
                ring_copy(axis, t, way, 1 - way).wait_recv()
        for axis in range(2):
            for way in range(2):
                ring_copy(axis, t, way, 2).wait_recv()

    def ring_sent(t):
        for axis in range(2):
            for way in range(2):
                for kind in range(3):
                    ring_copy(axis, t, way, kind).wait_send()

    def core_copy(n, b):
        q = sum(len(blocks) for _, blocks in GROUPS[:n]) + b
        return pltpu.make_async_remote_copy(
            src_ref=cx[n].at[b, 1 - core],
            dst_ref=cr[n].at[b],
            send_sem=core_send.at[q],
            recv_sem=core_recv.at[q],
            device_id=other_core,
            device_id_type=MESH,
        )

    def z_copy(n, d):
        q = 7 * n + d - 1
        return pltpu.make_async_remote_copy(
            src_ref=zs[n].at[z_at(d)],
            dst_ref=zr[n].at[d - 1],
            send_sem=z_send.at[q],
            recv_sem=z_recv.at[q],
            device_id=z_dev(d),
            device_id_type=MESH,
        )

    def multiply(n):
        for b, (i, j) in enumerate(GROUPS[n][1]):
            left = jnp.concatenate(
                [lg[s, CR * i : CR * i + CR, :] for s in range(8)], axis=1
            )
            right = ug[j][...].reshape(2048, CW)
            cx[n][b] = jnp.dot(left, right, preferred_element_type=F32).reshape(
                2, CR // 2, CW
            )
            core_copy(n, b).start()

    def scatter(n):
        for b in range(len(GROUPS[n][1])):
            core_copy(n, b).wait()
            total = cx[n][b, core] + cr[n][b]
            cx[n][b, core] = total
            zs[n][:, H * b : H * b + H, :] = total.reshape(8, H, CW).astype(BF16)
        for d in (4, 3, 5, 2, 6, 1, 7):
            z_copy(n, d).start()

    def finish(n):
        for d in (1, 7, 2, 6, 3, 5, 4):
            z_copy(n, d).wait()
        for b, (i, j) in enumerate(GROUPS[n][1]):
            total = cx[n][b, core, pl.ds(pl.multiple_of(H * z, H), H), :]
            for d in range(1, 8):
                total += zr[n][d - 1, H * b : H * b + H, :].astype(F32)
            out_ref[H * i : H * i + H, CW * j : CW * j + CW] = total

    of_phase = [[n for n, (p, _) in enumerate(GROUPS) if p == q] for q in range(PARTS)]

    loads[0].wait()
    loads[1].wait()
    lower(0)
    pl.semaphore_wait(barrier, len(peers))
    direct(0, 0)
    direct(1, 0)
    direct(0, 1)
    lower(1)
    direct(1, 1)
    for t in range(2, PARTS):
        lower(t)
    for cp in loads[2:]:
        cp.wait()
    for t in range(PARTS + 1):
        if t < PARTS:
            forward(t)
            if t + 2 < PARTS:
                direct(0, t + 2)
                direct(1, t + 2)
        if t >= 2:
            for n in of_phase[t - 2]:
                scatter(n)
        if t >= 1:
            rest(t - 1)
            for n in of_phase[t - 1]:
                multiply(n)
            ring_sent(t - 1)
    for n in of_phase[PARTS - 1]:
        scatter(n)
    for n in range(len(GROUPS)):
        finish(n)


def local(col_panels, row_panels, diag_inverse, live, schur_block):
    panels = col_panels[0].reshape(2, 8, 2, 64, 256)
    count = [len(blocks) for _, blocks in GROUPS]
    any_spec = pl.BlockSpec(memory_space=pl.ANY)
    summed = pl.pallas_call(
        kernel,
        out_shape=jax.ShapeDtypeStruct((64, 1024), F32),
        in_specs=[pl.BlockSpec(memory_space=pltpu.SMEM)] + [any_spec] * 3,
        out_specs=pl.BlockSpec(memory_space=pltpu.VMEM),
        scratch_shapes=[
            pltpu.VMEM((2, 8, 2, 64, 256), BF16),
            pltpu.VMEM((2, 256, 256), BF16),
            pltpu.VMEM((8, 1024, 256), BF16),
        ]
        + [pltpu.VMEM((8, 256, CW), BF16) for _ in range(PARTS)]
        + [pltpu.VMEM((k, 2, CR // 2, CW), F32) for k in count]
        + [pltpu.VMEM((k, CR // 2, CW), F32) for k in count]
        + [pltpu.VMEM((8, H * k, CW), BF16) for k in count]
        + [pltpu.VMEM((7, H * k, CW), BF16) for k in count]
        + [
            pltpu.SemaphoreType.DMA((2 + PARTS,)),
            pltpu.SemaphoreType.DMA((12 * PARTS,)),
            pltpu.SemaphoreType.DMA((12 * PARTS,)),
            pltpu.SemaphoreType.DMA((sum(count),)),
            pltpu.SemaphoreType.DMA((sum(count),)),
            pltpu.SemaphoreType.DMA((7 * len(count),)),
            pltpu.SemaphoreType.DMA((7 * len(count),)),
        ],
        compiler_params=pltpu.CompilerParams(
            collective_id=0, has_side_effects=True, vmem_limit_bytes=56 << 20
        ),
        name="schur_update",
    )(live, panels, row_panels[0], diag_inverse[0])
    return schur_block - summed


def solution(mesh):
    placed = (
        P("gz", "col", "row", None),
        P("gz", "row", None, "col"),
        P("gz", "col", None, None),
        P("gz"),
        P(("row", "gz"), "col"),
    )
    return jax.shard_map(
        local, mesh=mesh, in_specs=placed, out_specs=P(("row", "gz"), "col"), check_vma=False
    )
```

time: 198 us -> 72.5 us (0.37); the launches traced: 195 us -> 72.3 us
  waiting for transfers between devices: 167 us -> 0 us
  Pallas kernels: 0 us -> 70 us
  between operations: 13.8 us -> 0.68 us
  matrix products: 12.4 us -> 0 us
    all_gather x2 -> x0, waiting for transfers between devices: 106 us -> none  [the longest x1 53.1 us: local(): lowers = lax.all_gather(owned, 'col', axis=0, tiled=True)]
    pallas_call x0 -> x1, Pallas kernels: none -> 70 us  [local(): pl.pallas_call(kernel, out_shape=jax.ShapeDtypeStruct((64, 1024), F32), i...]
    reduce_scatter x1 -> x0, waiting for transfers between devices: 60.1 us -> none  [local(): lax.psum_scatter(partial_sum, 'gz', scatter_dimension=0, tiled=True)]
    dot_general x2 -> x0, matrix products: 12.4 us -> none  [the longest x1 9.94 us: local(): jnp.einsum('srw,swc->rc', lowers, uppers, preferred_element_type=jnp.floa...]
  transfers between devices with their start and end apart: 3 -> 0, of which waited for: 3 -> 0; matrix products, arithmetic and copies ran while one was open for 1% -> 0% of each run, Pallas kernels for 0% -> 0%
where the time goes in v1:
time: 72.5 us; the launch traced here: 72.3 us
  Pallas kernels  70 us (97%)
  other arithmetic  1.68 us (2%)
    pallas_call x1, Pallas kernels, local(): pl.pallas_call(kernel, out_shape=jax.ShapeDtypeStruct((64, 1024), F32), i...  70 us
    sub x1, other arithmetic, local(): return schur_block - summed  1.68 us

profile of v1, /device:TPU:1, one launch (start us, length us, event | category | flops | bytes accessed | tf_op | source)
XLA Modules:
  0.0 72.3 jit_solution(8213662682084459074)
XLA Ops:
  0.7 0.0 copy-start
  0.7 70.0 %schur_update.1 = f32[64,1024]{1,0:T(8,128)} custom-call(s32[1]{0:T(128)S(6)} %copy.6.live_ref, bf16[2,8,2,64,256]{4,3,2,1,0:T(8,128)(2,1)} %bitcast.3, bf16[2,256,1024]{2,1,0:T(8,128)(2,1)} %bitcast.4, bf16[2,256,256]{2,1,0:T(8,128)(2,1)} %bitcast.5), custom_call_target="tpu_custom_call" | custom-call | tf_op jit(solution)/shard_map/schur_update/pallas_call | solution.py:239
  70.6 0.0 copy-done
  70.7 1.7 %sub.3 = f32[64,1024]{1,0:T(8,128)} subtract(f32[64,1024]{1,0:T(8,128)S(1)} %copy-done, f32[64,1024]{1,0:T(8,128)} %schur_update.1) | non-fusion elementwise | flops 65536 | bytes 786432 | tf_op jit(solution)/shard_map/sub | solution.py:268
Async XLA Ops:
  0.7 70.0 %copy-start = (f32[64,1024]{1,0:T(8,128)S(1)}, f32[64,1024]{1,0:T(8,128)}, u32[]{:S(2)}) copy-start(f32[64,1024]{1,0:T(8,128)} %param.9) | copy-start | bytes 786436

commit v2 on v1

v2 whole, which is shorter than its diff:
```python
import jax
import jax.numpy as jnp
from jax import lax
from jax.experimental import pallas as pl
from jax.experimental.pallas import tpu as pltpu
from jax.sharding import PartitionSpec as P

MESH = pl.DeviceIdType.MESH
F32 = jnp.float32
BF16 = jnp.bfloat16

HEIGHT = (16, 16, 8, 8, 8, 8)
WIDTH = (256, 256, 128, 128, 128, 128)
PARTS = len(WIDTH)
TOP = tuple(sum(HEIGHT[:t]) for t in range(PARTS))
LEFT = tuple(sum(WIDTH[:t]) for t in range(PARTS))

PRODUCTS = (
    ((0, 1, 0, 1),),
    ((1, 1, 0, 1), (1, 1, 1, 1), (0, 1, 1, 1)),
    ((2, 1, 0, 1), (2, 1, 1, 1), (0, 1, 2, 1), (1, 1, 2, 1)),
    ((3, 1, 0, 1), (3, 1, 1, 1), (0, 1, 3, 1), (1, 1, 3, 1), (2, 2, 2, 1), (2, 2, 3, 1)),
    ((4, 1, 0, 1), (4, 1, 1, 1), (0, 1, 4, 1), (1, 1, 4, 1), (4, 1, 2, 2), (2, 2, 4, 1)),
    ((5, 1, 0, 1), (5, 1, 1, 1), (0, 1, 5, 1), (1, 1, 5, 1)),
    ((5, 1, 2, 2), (2, 2, 5, 1), (4, 2, 4, 1), (4, 2, 5, 1)),
)
PHASE = (0, 1, 2, 3, 4, 5, 5)
GROUPS = len(PRODUCTS)
EARLY = (4, 5, 6)


def units_of(product):
    i, rows, j, columns = product
    row, col = TOP[i], LEFT[j]
    if HEIGHT[i] * rows == 16:
        return [
            ((row, col + k), (row + 8, col + k))
            for k in range(0, WIDTH[j] * columns, 128)
        ]
    return [((row, col), (row, col + 128))]


UNITS = tuple([u for product in group for u in units_of(product)] for group in PRODUCTS)


def first_unit(n, b):
    return sum(len(units_of(product)) for product in PRODUCTS[n][:b])


def kernel(live_ref, x_hbm, u_hbm, d_hbm, out_ref, *scr):
    scr = list(scr)
    xs, dg, lg = scr[:3]
    del scr[:3]
    ug = [scr.pop(0) for _ in range(PARTS)]
    cx = [scr.pop(0) for _ in range(GROUPS)]
    cr = [scr.pop(0) for _ in range(GROUPS)]
    zs = [scr.pop(0) for _ in range(GROUPS)]
    zr = [scr.pop(0) for _ in range(GROUPS)]
    load_sem, ring_send, ring_recv, core_send, core_recv, z_send, z_recv = scr

    r, c, g = lax.axis_index("row"), lax.axis_index("col"), lax.axis_index("gz")
    z, core = lax.div(g, 2), lax.rem(g, 2)
    me = (r, c)

    def along(axis, d):
        if axis == 0:
            return (lax.rem(r + 4 + d, 4), c, g)
        return (r, lax.rem(c + 4 + d, 4), g)

    other_core = (r, c, 2 * z + 1 - core)

    def z_at(d):
        return lax.rem(z + d, 8)

    def z_dev(d):
        return (r, c, 2 * z_at(d) + core)

    barrier = pltpu.get_barrier_semaphore()
    peers = [along(a, d) for a in (0, 1) for d in (1, -1)]
    peers += [other_core] + [z_dev(d) for d in range(1, 8)]
    for dev in peers:
        pl.semaphore_signal(barrier, inc=1, device_id=dev, device_id_type=MESH)

    loads = [
        pltpu.make_async_copy(d_hbm, dg, load_sem.at[0]),
        pltpu.make_async_copy(x_hbm, xs, load_sem.at[1]),
    ]
    for t in range(PARTS):
        loads.append(
            pltpu.make_async_copy(
                u_hbm.at[:, :, pl.ds(LEFT[t], WIDTH[t])],
                ug[t].at[pl.ds(2 * r, 2)],
                load_sem.at[2 + t],
            )
        )
    for cp in loads:
        cp.start()

    def lower(t):
        for s in range(2):
            keep = jnp.where(2 * c + s < live_ref[0], 1.0, 0.0).astype(F32)
            halves = [
                xs[s, :, par, TOP[t] : TOP[t] + 16, :].reshape(128, 256)
                for par in range(2)
            ]
            prod = keep * jnp.dot(
                jnp.concatenate(halves, axis=0), dg[s], preferred_element_type=F32
            )
            slot = 2 * c + s
            if HEIGHT[t] == 16:
                lg[slot, 16 * TOP[t] : 16 * TOP[t] + 256, :] = prod.astype(BF16)
            else:
                prod = prod.reshape(16, 16, 256)
                for k in range(2):
                    at = 16 * TOP[t + k]
                    lg[slot, at : at + 128, :] = (
                        prod[:, 8 * k : 8 * k + 8, :].reshape(128, 256).astype(BF16)
                    )

    def piece(axis, slot, t):
        if axis == 0:
            return ug[t].at[slot]
        return lg.at[slot, pl.ds(16 * TOP[t], 16 * HEIGHT[t])]

    copies = {}

    def ring_copy(axis, t, way, kind):
        key = (axis, t, way, kind)
        if key not in copies:
            d = 1 if way == 0 else -1
            if kind < 2:
                slot = 2 * me[axis] + kind
            else:
                slot = 2 * lax.rem(me[axis] + 4 - d, 4) + way
            sem = ((axis * PARTS + t) * 2 + way) * 3 + kind
            src = dst = piece(axis, slot, t)
            if axis == 0 and kind < 2:
                src = u_hbm.at[kind, :, pl.ds(LEFT[t], WIDTH[t])]
            copies[key] = pltpu.make_async_remote_copy(
                src_ref=src,
                dst_ref=dst,
                send_sem=ring_send.at[sem],
                recv_sem=ring_recv.at[sem],
                device_id=along(axis, d),
                device_id_type=MESH,
            )
        return copies[key]

    def first(axis, t):
        for way in range(2):
            ring_copy(axis, t, way, way).start()

    def second(axis, t):
        for way in range(2):
            ring_copy(axis, t, way, 1 - way).start()

    def forward(t):
        for axis in range(2):
            for way in range(2):
                ring_copy(axis, t, way, way).wait_recv()
                ring_copy(axis, t, way, 2).start()
        for axis in range(2):
            if t + 1 < PARTS:
                second(axis, t + 1)
            if t + 2 < PARTS:
                first(axis, t + 2)

    def neighbours(t):
        for axis in range(2):
            for way in range(2):
                ring_copy(axis, t, way, 1 - way).wait_recv()

    def rest(t):
        if PHASE.index(t) not in EARLY:
            neighbours(t)
        for axis in range(2):
            for way in range(2):
                ring_copy(axis, t, way, 2).wait_recv()

    def ring_sent(t):
        for axis in range(2):
            for way in range(2):
                for kind in range(3):
                    ring_copy(axis, t, way, kind).wait_send()

    def core_copy(n, b):
        q = sum(len(group) for group in PRODUCTS[:n]) + b
        at = pl.ds(first_unit(n, b), len(units_of(PRODUCTS[n][b])))
        return pltpu.make_async_remote_copy(
            src_ref=cx[n].at[1 - core, at],
            dst_ref=cr[n].at[at],
            send_sem=core_send.at[q],
            recv_sem=core_recv.at[q],
            device_id=other_core,
            device_id_type=MESH,
        )

    def z_copy(n, d):
        q = 7 * n + d - 1
        return pltpu.make_async_remote_copy(
            src_ref=zs[n].at[z_at(d)],
            dst_ref=zr[n].at[d - 1],
            send_sem=z_send.at[q],
            recv_sem=z_recv.at[q],
            device_id=z_dev(d),
            device_id_type=MESH,
        )

    def factors(product, slots):
        i, many, j, columns = product
        rows = pl.ds(16 * TOP[i], 16 * HEIGHT[i] * many)
        left = jnp.concatenate([lg[s, rows, :] for s in slots], axis=1)
        right = [
            jnp.concatenate([ug[k][s] for s in slots], axis=0)
            for k in range(j, j + columns)
        ]
        return left, right[0] if columns == 1 else jnp.concatenate(right, axis=1)

    def by_units(product, prod):
        i, many, j, columns = product
        width = WIDTH[j] * columns
        if many == 2:
            prod = prod.reshape(2, 2, 8, 8, 128)
            return [jnp.concatenate([prod[0], prod[1]], axis=2)]
        if HEIGHT[i] == 16:
            prod = prod.reshape(2, 8, 16, width)
            return [prod[..., k : k + 128] for k in range(0, width, 128)]
        prod = prod.reshape(2, 8, 8, width)
        return [jnp.concatenate([prod[..., 0:128], prod[..., 128:256]], axis=2)]

    def slots_of(n, product, far):
        i, many, j, columns = product
        late = i + many - 1 == PHASE[n], j + columns - 1 == PHASE[n]
        if all(late):
            return None
        at = me[1] if late[0] else me[0]
        steps = (2,) if far else (0, 1, 3)
        return [2 * lax.rem(at + d, 4) + s for d in steps for s in range(2)]

    def begin(n):
        for b, product in enumerate(PRODUCTS[n]):
            slots = slots_of(n, product, False)
            if slots is not None:
                prod = jnp.dot(*factors(product, slots), preferred_element_type=F32)
                for k, unit in enumerate(by_units(product, prod)):
                    cx[n][:, first_unit(n, b) + k] = unit

    def multiply(n):
        for b, product in enumerate(PRODUCTS[n]):
            slots = slots_of(n, product, True) if n in EARLY else None
            prod = jnp.dot(
                *factors(product, range(8) if slots is None else slots),
                preferred_element_type=F32,
            )
            for k, unit in enumerate(by_units(product, prod)):
                u = first_unit(n, b) + k
                if slots is not None:
                    unit += cx[n][:, u]
                cx[n][:, u] = unit
            core_copy(n, b).start()

    def add_cores(n):
        for b in range(len(PRODUCTS[n])):
            core_copy(n, b).wait()
        for u in range(len(UNITS[n])):
            total = cx[n][core, u] + cr[n][u]
            cx[n][core, u] = total
            zs[n][:, 16 * u : 16 * u + 16, :] = total.astype(BF16)

    def scatter(n):
        add_cores(n)
        for d in (4, 3, 5, 2, 6, 1, 7):
            z_copy(n, d).start()

    def write(unit, total):
        for k, (row, col) in enumerate(unit):
            out_ref[row : row + 8, col : col + 128] = total[8 * k : 8 * k + 8, :]

    def finish(n):
        for d in (1, 7, 2, 6, 3, 5, 4):
            z_copy(n, d).wait()
        for u, unit in enumerate(UNITS[n]):
            total = cx[n][core, u, z]
            for d in range(1, 8):
                total += zr[n][d - 1, 16 * u : 16 * u + 16, :].astype(F32)
            write(unit, total)

    loads[0].wait()
    loads[1].wait()
    lower(0)
    lower(1)
    pl.semaphore_wait(barrier, len(peers))
    for axis in range(2):
        first(axis, 0)
    for axis in range(2):
        second(axis, 0)
    for axis in range(2):
        first(axis, 1)
    lower(2)
    lower(4)
    for cp in loads[2:]:
        cp.wait()

    forward(0)
    forward(1)
    rest(0)
    multiply(0)
    forward(2)
    scatter(0)
    ring_sent(0)
    rest(1)
    multiply(1)
    forward(3)
    scatter(1)
    rest(2)
    multiply(2)
    forward(4)
    scatter(2)
    ring_sent(1)
    rest(3)
    multiply(3)
    forward(5)
    neighbours(4)
    begin(4)
    scatter(3)
    rest(4)
    multiply(4)
    neighbours(5)
    begin(5)
    begin(6)
    scatter(4)
    rest(5)
    multiply(5)
    multiply(6)
    ring_sent(2)
    scatter(5)
    scatter(6)
    for t in range(3, PARTS):
        ring_sent(t)
    for n in range(GROUPS):
        finish(n)


def local(col_panels, row_panels, diag_inverse, live, schur_block):
    panels = col_panels[0].reshape(2, 8, 2, 64, 256)
    count = [len(units) for units in UNITS]
    products = sum(len(group) for group in PRODUCTS)
    hbm = pl.BlockSpec(memory_space=pltpu.HBM)

    summed = pl.pallas_call(
        kernel,
        out_shape=jax.ShapeDtypeStruct((64, 1024), F32),
        in_specs=[pl.BlockSpec(memory_space=pltpu.SMEM)] + [hbm] * 3,
        out_specs=pl.BlockSpec(memory_space=pltpu.VMEM),
        scratch_shapes=[
            pltpu.VMEM((2, 8, 2, 64, 256), BF16),
            pltpu.VMEM((2, 256, 256), BF16),
            pltpu.VMEM((8, 1024, 256), BF16),
        ]
        + [pltpu.VMEM((8, 256, w), BF16) for w in WIDTH]
        + [pltpu.VMEM((2, k, 8, 16, 128), F32) for k in count]
        + [pltpu.VMEM((k, 8, 16, 128), F32) for k in count]
        + [pltpu.VMEM((8, 16 * k, 128), BF16) for k in count]
        + [pltpu.VMEM((7, 16 * k, 128), BF16) for k in count]
        + [
            pltpu.SemaphoreType.DMA((2 + PARTS,)),
            pltpu.SemaphoreType.DMA((12 * PARTS,)),
            pltpu.SemaphoreType.DMA((12 * PARTS,)),
            pltpu.SemaphoreType.DMA((products,)),
            pltpu.SemaphoreType.DMA((products,)),
            pltpu.SemaphoreType.DMA((7 * GROUPS,)),
            pltpu.SemaphoreType.DMA((7 * GROUPS,)),
        ],
        compiler_params=pltpu.CompilerParams(
            collective_id=0, has_side_effects=True, vmem_limit_bytes=53 << 20
        ),
        name="schur_update",
    )(live, panels, row_panels[0], diag_inverse[0])
    return schur_block - summed


def solution(mesh):
    placed = (
        P("gz", "col", "row", None),
        P("gz", "row", None, "col"),
        P("gz", "col", None, None),
        P("gz"),
        P(("row", "gz"), "col"),
    )
    return jax.shard_map(
        local, mesh=mesh, in_specs=placed, out_specs=P(("row", "gz"), "col"), check_vma=False
    )
```

time: 72.5 us -> 64.1 us (0.88)
  Pallas kernels: 70 us -> 61.6 us
  other arithmetic: 1.68 us -> 0.73 us
  local copies, waits for them, and re-layouts: 0.01 us -> 0.95 us
    pallas_call x1, Pallas kernels: 70 us -> 61.6 us  [local(): pl.pallas_call(kernel, out_shape=jax.ShapeDtypeStruct((64, 1024), F32), i...]
    sub x1, other arithmetic: 1.68 us -> 0.73 us  [local(): return schur_block - summed]
    unnamed x2 -> x4, local copies, waits for them, and re-layouts: 0.01 us -> 0.95 us
where the time goes in v2:
time: 64.1 us; the launch traced here: 63.9 us
  Pallas kernels  61.6 us (96%)
  local copies, waits for them, and re-layouts  0.95 us (1%)
  other arithmetic  0.73 us (1%)
  between operations  0.68 us (1%)
    pallas_call x1, Pallas kernels, local(): pl.pallas_call(kernel, out_shape=jax.ShapeDtypeStruct((64, 1024), F32), i...  61.6 us

profile of v2, /device:TPU:1, one launch (start us, length us, event | category | flops | bytes accessed | tf_op | source)
XLA Modules:
  0.0 63.9 jit_solution(10516459550052822401)
XLA Ops:
  0.7 0.0 copy-start
  0.7 0.9 %copy-done = bf16[1,2,256,256]{3,2,1,0:T(8,128)(2,1)S(1)} copy-done((bf16[1,2,256,256]{3,2,1,0:T(8,128)(2,1)S(1)}, bf16[1,2,256,256]{3,2,1,0:T(8,128)(2,1)}, u32[]{:S(2)}) %copy-start) | copy-done | bytes 262168
  1.6 0.0 copy-start.1
  1.6 61.6 %schur_update.1 = f32[64,1024]{1,0:T(8,128)S(1)} custom-call(s32[1]{0:T(128)S(6)} %copy.6.live_ref, bf16[2,8,2,64,256]{4,3,2,1,0:T(8,128)(2,1)} %bitcast.4, bf16[2,256,1024]{2,1,0:T(8,128)(2,1)} %bitcast.5, bf16[2,256,256]{2,1,0:T(8,128)(2,1)S(1)} %bitcast.3), custom_call_target="tpu_custom_call" | custom-call | tf_op jit(solution)/shard_map/schur_update/pallas_call | solution.py:350
  63.2 0.0 copy-done.1
  63.2 0.7 %sub.3 = f32[64,1024]{1,0:T(8,128)} subtract(f32[64,1024]{1,0:T(8,128)S(1)} %copy-done.1, f32[64,1024]{1,0:T(8,128)S(1)} %schur_update.1) | non-fusion elementwise | flops 65536 | bytes 786432 | tf_op jit(solution)/shard_map/sub | solution.py:379
Async XLA Ops:
  0.7 1.0 %copy-start = (bf16[1,2,256,256]{3,2,1,0:T(8,128)(2,1)S(1)}, bf16[1,2,256,256]{3,2,1,0:T(8,128)(2,1)}, u32[]{:S(2)}) copy-start(bf16[1,2,256,256]{3,2,1,0:T(8,128)(2,1)} %param.7) | copy-start | bytes 786436
  1.6 61.6 %copy-start.1 = (f32[64,1024]{1,0:T(8,128)S(1)}, f32[64,1024]{1,0:T(8,128)}, u32[]{:S(2)}) copy-start(f32[64,1024]{1,0:T(8,128)} %param.9) | copy-start | bytes 786436

commit v3 on v2

--- a/solution.py
+++ b/solution.py
@@ -21,12 +21,12 @@
     ((2, 1, 0, 1), (2, 1, 1, 1), (0, 1, 2, 1), (1, 1, 2, 1)),
     ((3, 1, 0, 1), (3, 1, 1, 1), (0, 1, 3, 1), (1, 1, 3, 1), (2, 2, 2, 1), (2, 2, 3, 1)),
     ((4, 1, 0, 1), (4, 1, 1, 1), (0, 1, 4, 1), (1, 1, 4, 1), (4, 1, 2, 2), (2, 2, 4, 1)),
-    ((5, 1, 0, 1), (5, 1, 1, 1), (0, 1, 5, 1), (1, 1, 5, 1)),
-    ((5, 1, 2, 2), (2, 2, 5, 1), (4, 2, 4, 1), (4, 2, 5, 1)),
+    ((5, 1, 0, 1), (5, 1, 1, 1), (0, 1, 5, 1), (1, 1, 5, 1), (5, 1, 2, 2), (2, 2, 5, 1), (4, 2, 4, 1), (4, 2, 5, 1)),
 )
-PHASE = (0, 1, 2, 3, 4, 5, 5)
+PHASE = (0, 1, 2, 3, 4, 5)
 GROUPS = len(PRODUCTS)
-EARLY = (4, 5, 6)
+RELAYED = (3, 4, 5)
+EARLY = (4, 5)
 
 
 def units_of(product):
@@ -75,28 +75,31 @@
     def z_dev(d):
         return (r, c, 2 * z_at(d) + core)
 
+    def load(n, src, dst):
+        return pltpu.make_async_copy(src, dst, load_sem.at[n])
+
+    load_d = load(0, d_hbm, dg)
+    load_x = [
+        load(1 + k, x_hbm.at[:, :, :, pl.ds(16 * k, 16)], xs.at[:, :, :, pl.ds(16 * k, 16)])
+        for k in range(4)
+    ]
+    load_u = [
+        load(5 + t, u_hbm.at[:, :, pl.ds(LEFT[t], WIDTH[t])], ug[t].at[pl.ds(2 * r, 2)])
+        for t in range(PARTS)
+    ]
+    load_d.start()
+    load_x[0].start()
+
     barrier = pltpu.get_barrier_semaphore()
     peers = [along(a, d) for a in (0, 1) for d in (1, -1)]
     peers += [other_core] + [z_dev(d) for d in range(1, 8)]
     for dev in peers:
         pl.semaphore_signal(barrier, inc=1, device_id=dev, device_id_type=MESH)
-
-    loads = [
-        pltpu.make_async_copy(d_hbm, dg, load_sem.at[0]),
-        pltpu.make_async_copy(x_hbm, xs, load_sem.at[1]),
-    ]
-    for t in range(PARTS):
-        loads.append(
-            pltpu.make_async_copy(
-                u_hbm.at[:, :, pl.ds(LEFT[t], WIDTH[t])],
-                ug[t].at[pl.ds(2 * r, 2)],
-                load_sem.at[2 + t],
-            )
-        )
-    for cp in loads:
+    for cp in load_x[1:] + load_u:
         cp.start()
 
     def lower(t):
+        load_x[TOP[t] // 16].wait()
         for s in range(2):
             keep = jnp.where(2 * c + s < live_ref[0], 1.0, 0.0).astype(F32)
             halves = [
@@ -158,11 +161,16 @@
         for axis in range(2):
             for way in range(2):
                 ring_copy(axis, t, way, way).wait_recv()
+        if t == PARTS - 3:
+            for axis in range(2):
+                first(axis, PARTS - 1)
+        for axis in range(2):
+            for way in range(2):
                 ring_copy(axis, t, way, 2).start()
         for axis in range(2):
             if t + 1 < PARTS:
                 second(axis, t + 1)
-            if t + 2 < PARTS:
+            if t + 2 < PARTS - 1:
                 first(axis, t + 2)
 
     def neighbours(t):
@@ -195,14 +203,23 @@
             device_id_type=MESH,
         )
 
-    def z_copy(n, d):
-        q = 7 * n + d - 1
+    def z_copy(n, m):
+        rows = 16 * len(UNITS[n])
+        at = pl.ds(0, rows)
+        to = of = m
+        if n in RELAYED:
+            kind, way = m // 2, m % 2
+            to, of = (1, 2, 1, 2)[kind], (3, 4, 1, 2)[kind]
+            if way:
+                to, of = 8 - to, 8 - of
+            if kind == 1:
+                at = pl.ds(rows // 2 * way, rows // 2)
         return pltpu.make_async_remote_copy(
-            src_ref=zs[n].at[z_at(d)],
-            dst_ref=zr[n].at[d - 1],
-            send_sem=z_send.at[q],
-            recv_sem=z_recv.at[q],
-            device_id=z_dev(d),
+            src_ref=zs[n].at[z_at(of), at],
+            dst_ref=zr[n].at[m, at],
+            send_sem=z_send.at[8 * n + m],
+            recv_sem=z_recv.at[8 * n + m],
+            device_id=z_dev(to),
             device_id_type=MESH,
         )
 
@@ -269,36 +286,50 @@
 
     def scatter(n):
         add_cores(n)
-        for d in (4, 3, 5, 2, 6, 1, 7):
-            z_copy(n, d).start()
+        for m in (2, 3, 0, 1, 4, 5) if n in RELAYED else (4, 3, 5, 2, 6, 1, 7):
+            z_copy(n, m).start()
+
+    def relay(n):
+        rows = 16 * len(UNITS[n])
+        for way in range(2):
+            z_copy(n, way).wait()
+            z_copy(n, 2 + way).wait()
+            dest = z_at(6 if way else 2)
+            total = cx[n][core, :, dest].reshape(rows, 128) + zr[n][way].astype(F32)
+            half = [slice(0, rows // 2), slice(rows // 2, rows)]
+            mine, other = half[way], half[1 - way]
+            more = zr[n][2 + way, mine, :].astype(F32)
+            zs[n][dest, mine, :] = (total[mine] + more).astype(BF16)
+            zs[n][dest, other, :] = total[other].astype(BF16)
+            z_copy(n, 6 + way).start()
 
     def write(unit, total):
         for k, (row, col) in enumerate(unit):
             out_ref[row : row + 8, col : col + 128] = total[8 * k : 8 * k + 8, :]
 
     def finish(n):
-        for d in (1, 7, 2, 6, 3, 5, 4):
-            z_copy(n, d).wait()
+        last = (4, 5, 6, 7) if n in RELAYED else (1, 7, 2, 6, 3, 5, 4)
+        for m in last:
+            z_copy(n, m).wait()
         for u, unit in enumerate(UNITS[n]):
             total = cx[n][core, u, z]
-            for d in range(1, 8):
-                total += zr[n][d - 1, 16 * u : 16 * u + 16, :].astype(F32)
+            for m in last:
+                total += zr[n][m, 16 * u : 16 * u + 16, :].astype(F32)
             write(unit, total)
 
-    loads[0].wait()
-    loads[1].wait()
+    load_d.wait()
     lower(0)
     lower(1)
     pl.semaphore_wait(barrier, len(peers))
-    for axis in range(2):
+    for axis in (1, 0):
         first(axis, 0)
-    for axis in range(2):
+    for axis in (1, 0):
         second(axis, 0)
-    for axis in range(2):
+    for axis in (1, 0):
         first(axis, 1)
     lower(2)
     lower(4)
-    for cp in loads[2:]:
+    for cp in load_u:
         cp.wait()
 
     forward(0)
@@ -317,9 +348,9 @@
     forward(4)
     scatter(2)
     ring_sent(1)
+    forward(5)
     rest(3)
     multiply(3)
-    forward(5)
     neighbours(4)
     begin(4)
     scatter(3)
@@ -327,22 +358,25 @@
     multiply(4)
     neighbours(5)
     begin(5)
-    begin(6)
     scatter(4)
     rest(5)
     multiply(5)
-    multiply(6)
+    relay(3)
     ring_sent(2)
     scatter(5)
-    scatter(6)
+    relay(4)
     for t in range(3, PARTS):
         ring_sent(t)
-    for n in range(GROUPS):
+    for n in range(3):
+        finish(n)
+    relay(5)
+    for n in range(3, GROUPS):
         finish(n)
 
 
 def local(col_panels, row_panels, diag_inverse, live, schur_block):
     panels = col_panels[0].reshape(2, 8, 2, 64, 256)
+    operands = panels, row_panels[0], diag_inverse[0]
     count = [len(units) for units in UNITS]
     products = sum(len(group) for group in PRODUCTS)
     hbm = pl.BlockSpec(memory_space=pltpu.HBM)
@@ -361,21 +395,21 @@
         + [pltpu.VMEM((2, k, 8, 16, 128), F32) for k in count]
         + [pltpu.VMEM((k, 8, 16, 128), F32) for k in count]
         + [pltpu.VMEM((8, 16 * k, 128), BF16) for k in count]
-        + [pltpu.VMEM((7, 16 * k, 128), BF16) for k in count]
+        + [pltpu.VMEM((8, 16 * k, 128), BF16) for k in count]
         + [
-            pltpu.SemaphoreType.DMA((2 + PARTS,)),
+            pltpu.SemaphoreType.DMA((5 + PARTS,)),
             pltpu.SemaphoreType.DMA((12 * PARTS,)),
             pltpu.SemaphoreType.DMA((12 * PARTS,)),
             pltpu.SemaphoreType.DMA((products,)),
             pltpu.SemaphoreType.DMA((products,)),
-            pltpu.SemaphoreType.DMA((7 * GROUPS,)),
-            pltpu.SemaphoreType.DMA((7 * GROUPS,)),
+            pltpu.SemaphoreType.DMA((8 * GROUPS,)),
+            pltpu.SemaphoreType.DMA((8 * GROUPS,)),
         ],
         compiler_params=pltpu.CompilerParams(
-            collective_id=0, has_side_effects=True, vmem_limit_bytes=53 << 20
+            collective_id=0, has_side_effects=True, vmem_limit_bytes=40 << 20
         ),
         name="schur_update",
-    )(live, panels, row_panels[0], diag_inverse[0])
+    )(live, *[pltpu.with_memory_space_constraint(a, pltpu.HBM) for a in operands])
     return schur_block - summed
 
 

time: 64.1 us -> 61.7 us (0.963)
  Pallas kernels: 61.6 us -> 60.1 us
  local copies, waits for them, and re-layouts: 0.95 us -> 0.01 us
    pallas_call x1, Pallas kernels: 61.6 us -> 60.1 us  [local(): pl.pallas_call(kernel, out_shape=jax.ShapeDtypeStruct((64, 1024), F32), i...]
    unnamed x4 -> x2, local copies, waits for them, and re-layouts: 0.95 us -> 0.01 us
where the time goes in v3:
time: 61.7 us; the launch traced here: 61.6 us
  Pallas kernels  60.1 us (97%)
  other arithmetic  0.73 us (1%)
  between operations  0.68 us (1%)
    pallas_call x1, Pallas kernels, local(): pl.pallas_call(kernel, out_shape=jax.ShapeDtypeStruct((64, 1024), F32), i...  60.1 us

profile of v3, /device:TPU:1, one launch (start us, length us, event | category | flops | bytes accessed | tf_op | source)
XLA Modules:
  0.0 61.6 jit_solution(7675065305337300609)
XLA Ops:
  0.7 0.0 copy-start
  0.7 60.1 %schur_update.1 = f32[64,1024]{1,0:T(8,128)S(1)} custom-call(s32[1]{0:T(128)S(6)} %copy.6.live_ref, bf16[2,8,2,64,256]{4,3,2,1,0:T(8,128)(2,1)} %bitcast.3, bf16[2,256,1024]{2,1,0:T(8,128)(2,1)} %bitcast.4, bf16[2,256,256]{2,1,0:T(8,128)(2,1)} %bitcast.5), custom_call_target="tpu_custom_call" | custom-call | tf_op jit(solution)/shard_map/schur_update/pallas_call | solution.py:384
  60.8 0.0 copy-done
  60.8 0.7 %sub.3 = f32[64,1024]{1,0:T(8,128)} subtract(f32[64,1024]{1,0:T(8,128)S(1)} %copy-done, f32[64,1024]{1,0:T(8,128)S(1)} %schur_update.1) | non-fusion elementwise | flops 65536 | bytes 786432 | tf_op jit(solution)/shard_map/sub | solution.py:413
Async XLA Ops:
  0.7 60.2 %copy-start = (f32[64,1024]{1,0:T(8,128)S(1)}, f32[64,1024]{1,0:T(8,128)}, u32[]{:S(2)}) copy-start(f32[64,1024]{1,0:T(8,128)} %param.9) | copy-start | bytes 786436

commit v4 on v3

--- a/solution.py
+++ b/solution.py
@@ -9,35 +9,36 @@
 F32 = jnp.float32
 BF16 = jnp.bfloat16
 
-HEIGHT = (16, 16, 8, 8, 8, 8)
-WIDTH = (256, 256, 128, 128, 128, 128)
+HEIGHT = (32, 8, 8, 8, 8)
+WIDTH = (512, 128, 128, 128, 128)
 PARTS = len(WIDTH)
 TOP = tuple(sum(HEIGHT[:t]) for t in range(PARTS))
 LEFT = tuple(sum(WIDTH[:t]) for t in range(PARTS))
 
 PRODUCTS = (
     ((0, 1, 0, 1),),
-    ((1, 1, 0, 1), (1, 1, 1, 1), (0, 1, 1, 1)),
-    ((2, 1, 0, 1), (2, 1, 1, 1), (0, 1, 2, 1), (1, 1, 2, 1)),
-    ((3, 1, 0, 1), (3, 1, 1, 1), (0, 1, 3, 1), (1, 1, 3, 1), (2, 2, 2, 1), (2, 2, 3, 1)),
-    ((4, 1, 0, 1), (4, 1, 1, 1), (0, 1, 4, 1), (1, 1, 4, 1), (4, 1, 2, 2), (2, 2, 4, 1)),
-    ((5, 1, 0, 1), (5, 1, 1, 1), (0, 1, 5, 1), (1, 1, 5, 1), (5, 1, 2, 2), (2, 2, 5, 1), (4, 2, 4, 1), (4, 2, 5, 1)),
+    ((1, 1, 0, 1), (0, 1, 1, 1)),
+    ((2, 1, 0, 1), (0, 1, 2, 1), (1, 2, 1, 1), (1, 2, 2, 1)),
+    ((3, 1, 0, 1), (0, 1, 3, 1), (3, 1, 1, 2), (1, 2, 3, 1)),
+    ((4, 1, 0, 1), (0, 1, 4, 1), (4, 1, 1, 2), (1, 2, 4, 1), (3, 2, 3, 1), (3, 2, 4, 1)),
 )
-PHASE = (0, 1, 2, 3, 4, 5)
+PHASE = (0, 1, 2, 3, 4)
 GROUPS = len(PRODUCTS)
-RELAYED = (3, 4, 5)
-EARLY = (4, 5)
+RELAYED = (3, 4)
+EARLY = (3, 4)
 
 
 def units_of(product):
     i, rows, j, columns = product
-    row, col = TOP[i], LEFT[j]
-    if HEIGHT[i] * rows == 16:
-        return [
-            ((row, col + k), (row + 8, col + k))
-            for k in range(0, WIDTH[j] * columns, 128)
-        ]
-    return [((row, col), (row, col + 128))]
+    row, col, width = TOP[i], LEFT[j], WIDTH[j] * columns
+    height = HEIGHT[i] * rows
+    if height == 8:
+        return [((row, col + k), (row, col + k + 128)) for k in range(0, width, 256)]
+    return [
+        ((row + a, col + k), (row + a + 8, col + k))
+        for a in range(0, height, 16)
+        for k in range(0, width, 128)
+    ]
 
 
 UNITS = tuple([u for product in group for u in units_of(product)] for group in PRODUCTS)
@@ -99,19 +100,21 @@
         cp.start()
 
     def lower(t):
-        load_x[TOP[t] // 16].wait()
+        tall = max(HEIGHT[t], 16)
+        for k in range(TOP[t] // 16, (TOP[t] + tall) // 16):
+            load_x[k].wait()
         for s in range(2):
             keep = jnp.where(2 * c + s < live_ref[0], 1.0, 0.0).astype(F32)
             halves = [
-                xs[s, :, par, TOP[t] : TOP[t] + 16, :].reshape(128, 256)
+                xs[s, :, par, TOP[t] : TOP[t] + tall, :].reshape(8 * tall, 256)
                 for par in range(2)
             ]
             prod = keep * jnp.dot(
                 jnp.concatenate(halves, axis=0), dg[s], preferred_element_type=F32
             )
             slot = 2 * c + s
-            if HEIGHT[t] == 16:
-                lg[slot, 16 * TOP[t] : 16 * TOP[t] + 256, :] = prod.astype(BF16)
+            if HEIGHT[t] == tall:
+                lg[slot, 16 * TOP[t] : 16 * (TOP[t] + tall), :] = prod.astype(BF16)
             else:
                 prod = prod.reshape(16, 16, 256)
                 for k in range(2):
@@ -161,17 +164,13 @@
         for axis in range(2):
             for way in range(2):
                 ring_copy(axis, t, way, way).wait_recv()
-        if t == PARTS - 3:
-            for axis in range(2):
-                first(axis, PARTS - 1)
-        for axis in range(2):
-            for way in range(2):
+                if t == PARTS - 3:
+                    ring_copy(axis, PARTS - 1, way, way).start()
                 ring_copy(axis, t, way, 2).start()
-        for axis in range(2):
-            if t + 1 < PARTS:
-                second(axis, t + 1)
-            if t + 2 < PARTS - 1:
-                first(axis, t + 2)
+                if t + 1 < PARTS:
+                    ring_copy(axis, t + 1, way, 1 - way).start()
+                if t + 2 < PARTS - 1:
+                    ring_copy(axis, t + 2, way, way).start()
 
     def neighbours(t):
         for axis in range(2):
@@ -239,11 +238,18 @@
         if many == 2:
             prod = prod.reshape(2, 2, 8, 8, 128)
             return [jnp.concatenate([prod[0], prod[1]], axis=2)]
-        if HEIGHT[i] == 16:
-            prod = prod.reshape(2, 8, 16, width)
-            return [prod[..., k : k + 128] for k in range(0, width, 128)]
-        prod = prod.reshape(2, 8, 8, width)
-        return [jnp.concatenate([prod[..., 0:128], prod[..., 128:256]], axis=2)]
+        height = HEIGHT[i]
+        prod = prod.reshape(2, 8, height, width)
+        if height == 8:
+            return [
+                jnp.concatenate([prod[..., k : k + 128], prod[..., k + 128 : k + 256]], axis=2)
+                for k in range(0, width, 256)
+            ]
+        return [
+            prod[:, :, a : a + 16, k : k + 128]
+            for a in range(0, height, 16)
+            for k in range(0, width, 128)
+        ]
 
     def slots_of(n, product, far):
         i, many, j, columns = product
@@ -327,8 +333,7 @@
         second(axis, 0)
     for axis in (1, 0):
         first(axis, 1)
-    lower(2)
-    lower(4)
+    lower(3)
     for cp in load_u:
         cp.wait()
 
@@ -338,17 +343,17 @@
     multiply(0)
     forward(2)
     scatter(0)
-    ring_sent(0)
     rest(1)
     multiply(1)
     forward(3)
     scatter(1)
+    ring_sent(0)
+    forward(4)
     rest(2)
     multiply(2)
-    forward(4)
+    neighbours(3)
+    begin(3)
     scatter(2)
-    ring_sent(1)
-    forward(5)
     rest(3)
     multiply(3)
     neighbours(4)
@@ -356,20 +361,14 @@
     scatter(3)
     rest(4)
     multiply(4)
-    neighbours(5)
-    begin(5)
+    ring_sent(1)
     scatter(4)
-    rest(5)
-    multiply(5)
     relay(3)
-    ring_sent(2)
-    scatter(5)
-    relay(4)
-    for t in range(3, PARTS):
+    for t in range(2, PARTS):
         ring_sent(t)
     for n in range(3):
         finish(n)
-    relay(5)
+    relay(4)
     for n in range(3, GROUPS):
         finish(n)
 

time: 61.7 us -> 61.2 us (level)
  no operation moved by 1% of the time
where the time goes in v4:
time: 61.2 us; the launch traced here: 61.1 us
  Pallas kernels  59.7 us (98%)
  other arithmetic  0.73 us (1%)
  between operations  0.68 us (1%)
    pallas_call x1, Pallas kernels, local(): pl.pallas_call(kernel, out_shape=jax.ShapeDtypeStruct((64, 1024), F32), i...  59.7 us

profile of v4, /device:TPU:1, one launch (start us, length us, event | category | flops | bytes accessed | tf_op | source)
XLA Modules:
  0.0 61.1 jit_solution(9105597590046093928)
XLA Ops:
  0.7 0.0 copy-start
  0.7 59.7 %schur_update.1 = f32[64,1024]{1,0:T(8,128)S(1)} custom-call(s32[1]{0:T(128)S(6)} %copy.6.live_ref, bf16[2,8,2,64,256]{4,3,2,1,0:T(8,128)(2,1)} %bitcast.3, bf16[2,256,1024]{2,1,0:T(8,128)(2,1)} %bitcast.4, bf16[2,256,256]{2,1,0:T(8,128)(2,1)} %bitcast.5), custom_call_target="tpu_custom_call" | custom-call | tf_op jit(solution)/shard_map/schur_update/pallas_call | solution.py:383
  60.3 0.0 copy-done
  60.3 0.7 %sub.3 = f32[64,1024]{1,0:T(8,128)} subtract(f32[64,1024]{1,0:T(8,128)S(1)} %copy-done, f32[64,1024]{1,0:T(8,128)S(1)} %schur_update.1) | non-fusion elementwise | flops 65536 | bytes 786432 | tf_op jit(solution)/shard_map/sub | solution.py:412
Async XLA Ops:
  0.7 59.7 %copy-start = (f32[64,1024]{1,0:T(8,128)S(1)}, f32[64,1024]{1,0:T(8,128)}, u32[]{:S(2)}) copy-start(f32[64,1024]{1,0:T(8,128)} %param.9) | copy-start | bytes 786436

commit v5 on v4

--- a/solution.py
+++ b/solution.py
@@ -9,23 +9,22 @@
 F32 = jnp.float32
 BF16 = jnp.bfloat16
 
-HEIGHT = (32, 8, 8, 8, 8)
-WIDTH = (512, 128, 128, 128, 128)
+HEIGHT = (32, 16, 8, 8)
+WIDTH = (512, 256, 128, 128)
 PARTS = len(WIDTH)
 TOP = tuple(sum(HEIGHT[:t]) for t in range(PARTS))
 LEFT = tuple(sum(WIDTH[:t]) for t in range(PARTS))
 
 PRODUCTS = (
     ((0, 1, 0, 1),),
-    ((1, 1, 0, 1), (0, 1, 1, 1)),
-    ((2, 1, 0, 1), (0, 1, 2, 1), (1, 2, 1, 1), (1, 2, 2, 1)),
-    ((3, 1, 0, 1), (0, 1, 3, 1), (3, 1, 1, 2), (1, 2, 3, 1)),
-    ((4, 1, 0, 1), (0, 1, 4, 1), (4, 1, 1, 2), (1, 2, 4, 1), (3, 2, 3, 1), (3, 2, 4, 1)),
+    ((1, 1, 0, 1), (0, 1, 1, 1), (1, 1, 1, 1)),
+    ((2, 1, 0, 1), (0, 1, 2, 1), (2, 1, 1, 1), (1, 1, 2, 1)),
+    ((3, 1, 0, 1), (0, 1, 3, 1), (3, 1, 1, 1), (1, 1, 3, 1), (2, 2, 2, 1), (2, 2, 3, 1)),
 )
-PHASE = (0, 1, 2, 3, 4)
+PHASE = (0, 1, 2, 3)
 GROUPS = len(PRODUCTS)
-RELAYED = (3, 4)
-EARLY = (3, 4)
+RELAYED = (1, 2, 3)
+EARLY = (1, 2, 3)
 
 
 def units_of(product):
@@ -164,9 +163,9 @@
         for axis in range(2):
             for way in range(2):
                 ring_copy(axis, t, way, way).wait_recv()
+                ring_copy(axis, t, way, 2).start()
                 if t == PARTS - 3:
                     ring_copy(axis, PARTS - 1, way, way).start()
-                ring_copy(axis, t, way, 2).start()
                 if t + 1 < PARTS:
                     ring_copy(axis, t + 1, way, 1 - way).start()
                 if t + 2 < PARTS - 1:
@@ -333,7 +332,7 @@
         second(axis, 0)
     for axis in (1, 0):
         first(axis, 1)
-    lower(3)
+    lower(2)
     for cp in load_u:
         cp.wait()
 
@@ -341,14 +340,17 @@
     forward(1)
     rest(0)
     multiply(0)
+    neighbours(1)
+    begin(1)
+    scatter(0)
     forward(2)
-    scatter(0)
     rest(1)
     multiply(1)
     forward(3)
+    ring_sent(0)
+    neighbours(2)
+    begin(2)
     scatter(1)
-    ring_sent(0)
-    forward(4)
     rest(2)
     multiply(2)
     neighbours(3)
@@ -356,21 +358,17 @@
     scatter(2)
     rest(3)
     multiply(3)
-    neighbours(4)
-    begin(4)
+    relay(1)
+    ring_sent(1)
     scatter(3)
-    rest(4)
-    multiply(4)
-    ring_sent(1)
-    scatter(4)
-    relay(3)
+    relay(2)
     for t in range(2, PARTS):
         ring_sent(t)
-    for n in range(3):
-        finish(n)
-    relay(4)
-    for n in range(3, GROUPS):
-        finish(n)
+    finish(0)
+    finish(1)
+    relay(3)
+    finish(2)
+    finish(3)
 
 
 def local(col_panels, row_panels, diag_inverse, live, schur_block):

time: 61.2 us -> 59.6 us (0.974)
  Pallas kernels: 59.7 us -> 57.8 us
    pallas_call x1, Pallas kernels: 59.7 us -> 57.8 us  [local(): pl.pallas_call(kernel, out_shape=jax.ShapeDtypeStruct((64, 1024), F32), i...]
where the time goes in v5:
time: 59.6 us; the launch traced here: 59.2 us
  Pallas kernels  57.8 us (97%)
  other arithmetic  0.73 us (1%)
  between operations  0.68 us (1%)
    pallas_call x1, Pallas kernels, local(): pl.pallas_call(kernel, out_shape=jax.ShapeDtypeStruct((64, 1024), F32), i...  57.8 us

profile of v5, /device:TPU:1, one launch (start us, length us, event | category | flops | bytes accessed | tf_op | source)
XLA Modules:
  0.0 59.2 jit_solution(8604696381359157807)
XLA Ops:
  0.7 0.0 copy-start
  0.7 57.8 %schur_update.1 = f32[64,1024]{1,0:T(8,128)S(1)} custom-call(s32[1]{0:T(128)S(6)} %copy.6.live_ref, bf16[2,8,2,64,256]{4,3,2,1,0:T(8,128)(2,1)} %bitcast.3, bf16[2,256,1024]{2,1,0:T(8,128)(2,1)} %bitcast.4, bf16[2,256,256]{2,1,0:T(8,128)(2,1)} %bitcast.5), custom_call_target="tpu_custom_call" | custom-call | tf_op jit(solution)/shard_map/schur_update/pallas_call | solution.py:381
  58.5 0.0 copy-done
  58.5 0.7 %sub.3 = f32[64,1024]{1,0:T(8,128)} subtract(f32[64,1024]{1,0:T(8,128)S(1)} %copy-done, f32[64,1024]{1,0:T(8,128)S(1)} %schur_update.1) | non-fusion elementwise | flops 65536 | bytes 786432 | tf_op jit(solution)/shard_map/sub | solution.py:410
Async XLA Ops:
  0.7 57.9 %copy-start = (f32[64,1024]{1,0:T(8,128)S(1)}, f32[64,1024]{1,0:T(8,128)}, u32[]{:S(2)}) copy-start(f32[64,1024]{1,0:T(8,128)} %param.9) | copy-start | bytes 786436
